TPU v7x, 512 devices: a whole 4x4x16 slice. The times are simulated.
512 devices in a mesh: tm: 16 (over z), space: 32 (over y, x, core).
Axes of the slice: x: 4, y: 4, z: 16, core: 2. Of those that a mesh axis runs over, the one named last changes fastest.
Arguments:
- displacements: bfloat16 [3, 16384, 16384], P(None, 'tm', 'space'), may hold values from -86.19596 to 86.19596
- block_place: int32 [128], replicated, may hold values from 0 to 127, as said below
- pair_list: int32 [384, 2], P('space'), may hold values from 0 to 127, as said below
- counts: int32 [32], P('space'), may hold values from 2 to 12, as said below
Outputs:
- covariance: float32 [384, 384, 384], P('tm', 'space')
Inputs may be any that keep to these rules, and one draw needn't show every extreme that they name: Block k is stored at position block_place[k] with block_place[k] // 4 equal to k // 4; on each device's 4 positions it is a permutation. `pair_list`: row i belongs to spatial device i // 12; its owner block lies on that device; its partner differs from the owner and lies on the same device or on one of the two devices beside it along space, cyclically; among a device's rows in use, the partners on the device before it are one single block, named at least once, and likewise for the device after it. `counts`: rows at or beyond the count are ignored; some device uses all 12 rows.
All inputs are finite; a program needn't handle non-finite values.
Results may differ from a plain program's by a relative error of at most 0.0035.
Values may be sent and summed in bfloat16 or wider, within the bound.
A program may use at most 128 MiB of HBM per device.

v0:
```python
import jax
import jax.numpy as jnp
from jax import lax
from jax.sharding import PartitionSpec as P

ATOMS_BLK = 128


def from_behind(value, axis, steps):
    count = lax.axis_size(axis)
    pairs = [(source, (source + steps) % count) for source in range(count)]
    return lax.ppermute(value, axis, pairs)


def wanted_block(rows_here, used_here, source, per_device):
    active = jnp.arange(rows_here.shape[0]) < used_here
    partner_block = rows_here[:, 1]
    matching_pairs = active & (partner_block // per_device == source)
    return jnp.max(jnp.where(matching_pairs, partner_block, -1))


def pick_block(blocks, block_place, wanted, device, per_device):
    position = jnp.clip(
        block_place[jnp.maximum(wanted, 0)] - device * per_device, 0, per_device - 1
    )
    chosen = blocks[position]
    return jnp.where(wanted >= 0, chosen, jnp.zeros_like(chosen))


def body(displacements, block_place, pair_list, counts):
    frames_dev = displacements.shape[1]
    atoms_dev = displacements.shape[2]
    n_tm = lax.axis_size("tm")
    n_space = lax.axis_size("space")
    per_device = atoms_dev // ATOMS_BLK
    span_width = 3 * ATOMS_BLK
    inverse_frames = 1.0 / (frames_dev * n_tm)
    frame_sums = jnp.sum(displacements, axis=1, dtype=jnp.float32)
    frame_mean = lax.psum(frame_sums, "tm") * inverse_frames
    centered = (displacements.astype(jnp.float32) - frame_mean[:, None, :]).astype(jnp.bfloat16)
    blocks = jnp.transpose(
        centered.reshape(3, frames_dev, per_device, ATOMS_BLK), (2, 1, 0, 3)
    ).reshape(per_device, frames_dev, span_width)
    device = lax.axis_index("space")
    before = (device + n_space - 1) % n_space
    partner_dev = pair_list[:, 1] // per_device
    own_partner = block_place[pair_list[:, 1]] - partner_dev * per_device
    rows_before, used_before = from_behind((pair_list, counts), "space", 1)
    rows_after, used_after = from_behind((pair_list, counts), "space", -1)
    send_after = pick_block(
        blocks,
        block_place,
        wanted_block(rows_after, used_after[0], device, per_device),
        device,
        per_device,
    )
    send_before = pick_block(
        blocks,
        block_place,
        wanted_block(rows_before, used_before[0], device, per_device),
        device,
        per_device,
    )
    left_block = from_behind(send_after, "space", 1)
    right_block = from_behind(send_before, "space", -1)
    block_pool = jnp.concatenate([blocks, left_block[None], right_block[None]], axis=0)
    partner_pos = jnp.where(
        partner_dev == device,
        own_partner,
        jnp.where(partner_dev == before, per_device, per_device + 1),
    )
    owner_pos = block_place[pair_list[:, 0]] - device * per_device
    slot_total = pair_list.shape[0]
    pair_count = counts[0]
    active = jnp.arange(slot_total) < pair_count
    weights = jnp.where(active, inverse_frames, 0.0).astype(jnp.float32)

    def pair_product(slot_index):
        owner_rows = block_pool[owner_pos[slot_index]]
        return lax.dot_general(
            owner_rows,
            block_pool[partner_pos[slot_index]],
            (((0,), (0,)), ((), ())),
            preferred_element_type=jnp.float32,
        )

    row_count = span_width // n_tm
    start_value = jnp.zeros((span_width, slot_total, span_width), jnp.float32)

    def accumulate(slot_index, accumulated):
        product = pair_product(slot_index) * weights[slot_index]
        return lax.dynamic_update_slice(
            accumulated, product[:, None, :], (jnp.int32(0), slot_index, jnp.int32(0))
        )

    summed = lax.psum(lax.fori_loop(0, slot_total, accumulate, start_value), "tm")
    result = lax.dynamic_slice_in_dim(summed, lax.axis_index("tm") * row_count, row_count, 0)
    return result


def solution(mesh):
    in_specs = (P(None, "tm", "space"), P(), P("space", None), P("space"))
    out_specs = P("tm", "space", None)
    return jax.shard_map(body, mesh=mesh, in_specs=in_specs, out_specs=out_specs, check_vma=False)
```

profile of v0, /device:TPU:30, one launch (start us, length us, event | category | flops | bytes accessed | tf_op | source)
XLA Modules:
  0.0 402.0 jit_solution(5085929860145891547)
XLA Ops:
  6.5 2.2 collective-permute-start.1
  8.7 2.2 collective-permute-start.4
  10.9 3.4 collective-permute-start
  14.3 5.5 %collective-permute-start.3 = (s32[1]{0:T(128)}, s32[1]{0:T(128)}, u32[]{:S(2)}, u32[]{:S(2)}) collective-permute-start(s32[1]{0:T(128)} %param.9), channel_id=1, source_target_pairs={{0,1},{1,2},{2,3},{3,4},{4,5},{5,6},{6,7},{7,8},{8,9},{9,10},{10,1... | collective-permute-start | bytes 20 | tf_op jit(solution)/shard_map/ppermute | solution.py:12
  20.5 3.2 copy.7
  24.2 36.3 %psum.14 = f32[3,512]{1,0:T(4,128)S(1)} all-reduce(f32[3,512]{1,0:T(4,128)S(1)} %convert_reduce_fusion), channel_id=1, replica_groups=mesh['tm'=16,'space'=32] {'tm'}, use_global_device_ids=true, to_apply=%region_1.0 | all-reduce | flops 1536 | bytes 12288 | tf_op jit(solution)/shard_map/psum | solution.py:39
  61.5 1.4 fusion.11
  64.3 1.3 fusion.10
  67.0 0.7 fusion.12
  69.0 1.3 select_bitcast_fusion.1
  70.3 1.9 collective-permute-start.2
  72.2 3.6 collective-permute-start.5
  75.9 0.7 gather_fusion.1
  76.6 0.7 gather_fusion
  77.3 6.6 %collective-permute-done.2 = bf16[1024,384]{0,1:T(8,128)(2,1)} collective-permute-done((bf16[1024,384]{0,1:T(8,128)(2,1)}, bf16[1024,384]{0,1:T(8,128)(2,1)}, u32[]{:S(2)}, u32[]{:S(2)}) %collective-permute-start.2) | collective-permute-done | bytes 786464 | tf_op jit(solution)/shard_map/ppermute | solution.py:12
  83.9 1.8 collective-permute-done.5
  85.7 3.5 pad_maximum_fusion
  89.2 6.7 %copy.9 = bf16[6,1024,384]{2,1,0:T(8,128)(2,1)} copy(bf16[6,1024,384]{1,2,0:T(8,128)(2,1)} %pad_maximum_fusion) | data formatting | bytes 9437184 | tf_op jit(solution)/shard_map/while | solution.py:96
  95.9 109.4 %while.13 = (s32[]{:T(128)}, f32[384,12,384]{2,0,1:T(8,128)}, s32[12]{0:T(128)S(1)}, bf16[6,1024,384]{2,1,0:T(8,128)(2,1)}, s32[12]{0:T(128)S(1)}, /*index=5*/f32[12]{0:T(128)S(1)}, s32[]{:T(128)}, s32[]{:T(128)}, s32[]{:T(128)}) while((s32[]{:T(128)}, f32[384,12,384]{2,0,1:T(8,128)}, s32[12]{0:T(128)S(1)}, bf16[6,1024,384]{2,1,0:T(8,128)(2,1)}, ...), condition=%wide.region_5.6_spmd, body=%wide.region_4.5_spmd.sunk | while | flops 302137344 | bytes 2163917 | solution.py:96
  95.9 0.6 dynamic_slice.76
  98.4 0.6 dynamic_slice.75
  101.0 0.6 dynamic_slice.77
  101.6 3.4 fusion.18
  105.0 0.6 dynamic_slice.76
  107.6 0.6 dynamic_slice.75
  110.1 0.6 dynamic_slice.77
  110.7 3.4 fusion.18
  116.7 0.6 dynamic_slice.75
  119.2 0.6 dynamic_slice.77
  119.8 3.5 fusion.18
  123.3 0.6 dynamic_slice.76
  125.8 0.6 dynamic_slice.75
  128.3 0.6 dynamic_slice.77
  129.0 3.5 fusion.18
  134.9 0.6 dynamic_slice.75
  137.5 0.6 dynamic_slice.77
  138.1 3.4 fusion.18
  144.0 0.6 dynamic_slice.75
  146.6 0.6 dynamic_slice.77
  147.2 3.4 fusion.18
  150.6 0.6 dynamic_slice.76
  153.1 0.6 dynamic_slice.75
  155.7 0.6 dynamic_slice.77
  156.3 3.4 fusion.18
  159.7 0.6 dynamic_slice.76
  162.3 0.6 dynamic_slice.75
  164.8 0.6 dynamic_slice.77
  165.4 3.4 fusion.18
  171.4 0.6 dynamic_slice.75
  173.9 0.6 dynamic_slice.77
  174.5 3.4 fusion.18
  180.5 0.6 dynamic_slice.75
  183.0 0.6 dynamic_slice.77
  183.6 3.5 fusion.18
  187.1 0.6 dynamic_slice.76
  189.6 0.6 dynamic_slice.75
  192.2 0.6 dynamic_slice.77
  192.8 3.4 fusion.18
  196.2 0.6 dynamic_slice.76
  198.7 0.6 dynamic_slice.75
  201.3 0.6 dynamic_slice.77
  201.9 3.4 fusion.18
  205.3 188.0 %all-reduce.2.cloned.1.call-done = f32[384,12,384]{2,0,1:T(8,128)} async-done(((f32[384,12,384]{2,0,1:T(8,128)}), f32[384,12,384]{2,0,1:T(8,128)}) %all-reduce.2.cloned.1.call-update) | async-done | bytes 7077904 | tf_op jit(solution)/shard_map/psum | solution.py:96
  393.3 1.8 constant_dynamic-slice_fusion
  (25 shorter events, 4.6 us)
Async XLA Ops:
  6.5 386.8 %all-reduce.2.cloned.1.call-start = ((), (), s32[]{:S(2)}) async-start(), calls=%async_computation | async-start | bytes 14155776 | tf_op jit(solution)/shard_map/psum | solution.py:96
  6.5 55.0 %collective-permute-start.1 = (s32[12,2]{0,1:T(2,128)}, s32[12,2]{0,1:T(2,128)S(1)}, u32[]{:S(2)}, u32[]{:S(2)}) collective-permute-start(s32[12,2]{0,1:T(2,128)} %param.8), channel_id=1, source_target_pairs={{0,31},{1,0},{2,1},{3,2},{4,3},{5,4},{6,5},{7,6},{8,7},{9,8},{10,9... | collective-permute-start | bytes 296 | tf_op jit(solution)/shard_map/ppermute | solution.py:12
  8.7 55.6 %collective-permute-start.4 = (s32[12,2]{0,1:T(2,128)}, s32[12,2]{0,1:T(2,128)S(1)}, u32[]{:S(2)}, u32[]{:S(2)}) collective-permute-start(s32[12,2]{0,1:T(2,128)} %param.8), channel_id=1, source_target_pairs={{0,1},{1,2},{2,3},{3,4},{4,5},{5,6},{6,7},{7,8},{8,9},{9,10},{10,1... | collective-permute-start | bytes 296 | tf_op jit(solution)/shard_map/ppermute | solution.py:12
  10.9 50.6 %collective-permute-start = (s32[1]{0:T(128)}, s32[1]{0:T(128)}, u32[]{:S(2)}, u32[]{:S(2)}) collective-permute-start(s32[1]{0:T(128)} %param.9), channel_id=1, source_target_pairs={{0,31},{1,0},{2,1},{3,2},{4,3},{5,4},{6,5},{7,6},{8,7},{9,8},{10,9... | collective-permute-start | bytes 20 | tf_op jit(solution)/shard_map/ppermute | solution.py:12
  14.3 50.0 %collective-permute-start.3 = (s32[1]{0:T(128)}, s32[1]{0:T(128)}, u32[]{:S(2)}, u32[]{:S(2)}) collective-permute-start(s32[1]{0:T(128)} %param.9), channel_id=1, source_target_pairs={{0,1},{1,2},{2,3},{3,4},{4,5},{5,6},{6,7},{7,8},{8,9},{9,10},{10,1... | collective-permute-start | bytes 20 | tf_op jit(solution)/shard_map/ppermute | solution.py:12
  61.1 5.9 %copy-start = (s32[128]{0:T(128)S(1)}, s32[128]{0:T(128)}, u32[]{:S(2)}) copy-start(s32[128]{0:T(128)} %param.7) | copy-start | bytes 1540
  61.1 14.8 %copy-start.1 = (s32[12,2]{0,1:T(2,128)S(1)}, s32[12,2]{0,1:T(2,128)}, u32[]{:S(2)}) copy-start(s32[12,2]{0,1:T(2,128)} %param.8) | copy-start | bytes 292
  70.3 13.6 %collective-permute-start.2 = (bf16[1024,384]{0,1:T(8,128)(2,1)}, bf16[1024,384]{0,1:T(8,128)(2,1)}, u32[]{:S(2)}, u32[]{:S(2)}) collective-permute-start(bf16[1024,384]{0,1:T(8,128)(2,1)} %get-tuple-element.139), channel_id=1, source_target_pairs={{0,1},{1,2},{2,3},{3,4},{4,5},{5,6},{6,7},{7,8},{8,9},{9,10},{10,1... | collective-permute-start | bytes 2359304 | tf_op jit(solution)/shard_map/ppermute | solution.py:12
  72.2 13.5 %collective-permute-start.5 = (bf16[1024,384]{0,1:T(8,128)(2,1)}, bf16[1024,384]{0,1:T(8,128)(2,1)}, u32[]{:S(2)}, u32[]{:S(2)}) collective-permute-start(bf16[1024,384]{0,1:T(8,128)(2,1)} %get-tuple-element.140), channel_id=1, source_target_pairs={{0,31},{1,0},{2,1},{3,2},{4,3},{5,4},{6,5},{7,6},{8,7},{9,8},{10,9... | collective-permute-start | bytes 2359304 | tf_op jit(solution)/shard_map/ppermute | solution.py:12
Sparse Core Ops, SparseCore 0:
  205.5 187.8 all-reduce.1
where the time goes:
time: 405 us; the launch traced here: 402 us
  waiting for transfers between devices  196 us (48%)
  loops' own time  46.1 us (11%)
  matrix products  41.2 us (10%)
  blocking collectives  36.3 us (9%)
  local copies, waits for them, and re-layouts  36.2 us (9%)
  starting transfers between devices  18.8 us (5%)
  between operations  18.3 us (5%)
  other arithmetic  8.67 us (2%)
    psum x1, waiting for transfers between devices, body(): lax.psum(lax.fori_loop(0, slot_total, accumulate, start_value), 'tm')  188 us
    another operation x1, loops' own time, body(): lax.fori_loop(0, slot_total, accumulate, start_value)  46.1 us
    dot_general x12, matrix products, pair_product(): lax.dot_general(owner_rows, block_pool[partner_pos[slot_index]], (((0,),...  41.2 us
    psum x1, blocking collectives, body(): frame_mean = lax.psum(frame_sums, 'tm') * inverse_frames  36.3 us
    ppermute x6, starting transfers between devices, from_behind(): return lax.ppermute(value, axis, pairs)  18.8 us
    ppermute x6, waiting for transfers between devices, from_behind(): return lax.ppermute(value, axis, pairs)  8.4 us
  transfers between devices with their start and end apart: 7, of which 3 were waited for; matrix products, arithmetic and copies ran while one was open for 2% of the time, Pallas kernels for 0%

commit v1 on v0

v1 whole, which is shorter than its diff:
```python
import functools

import jax
import jax.numpy as jnp
from jax import lax
from jax.experimental import pallas as pl
from jax.experimental.pallas import tpu as pltpu
from jax.sharding import PartitionSpec as P

MESH = pl.DeviceIdType.MESH
BLK = 128
COMPS = 3
SPAN = COMPS * BLK
GROUP = 2
EARLY = 4


def plan(here, per_device, n_space, place_ref, rows_ref, counts_ref, slot_ref, owner_ref, partner_ref):
    slots = rows_ref.shape[0]
    before = lax.rem(here + n_space - 1, n_space)
    after = lax.rem(here + 1, n_space)
    count = counts_ref[0]
    base = here * per_device
    own_used = jnp.int32(0)
    far_used = jnp.int32(0)
    want_before = jnp.int32(0)
    want_after = jnp.int32(0)
    keys, places, firsts, owners, partners = [], [], [], [], []
    for i in range(slots):
        o, q = rows_ref[i, 0], rows_ref[i, 1]
        q_dev = q // per_device
        o_pos = jnp.clip(place_ref[o] - base, 0, per_device - 1)
        q_pos = jnp.clip(place_ref[q] - q_dev * per_device, 0, per_device - 1)
        is_own = q_dev == here
        is_before = q_dev == before
        active = i < count
        key = o * (n_space * per_device) + q
        place = jnp.where(is_own, own_used, slots - 1 - far_used)
        first = jnp.where(active, jnp.int32(1), jnp.int32(0))
        for j in range(i):
            same = key == keys[j]
            place = jnp.where(same, places[j], place)
            first = jnp.where(same, 0, first)
        own_used = own_used + jnp.where(is_own, first, 0)
        far_used = far_used + jnp.where(is_own, 0, first)
        want_before = jnp.where(active & is_before, q_pos, want_before)
        want_after = jnp.where(active & (q_dev == after), q_pos, want_after)
        keys.append(key)
        places.append(place)
        firsts.append(first)
        owners.append(o_pos)
        partners.append(jnp.where(is_own, q_pos, jnp.where(is_before, per_device, per_device + 1)))
        slot_ref[i] = jnp.clip(place, 0, slots - 1)
    for k in range(slots):
        owner_k, partner_k = jnp.int32(0), jnp.int32(0)
        for i in range(slots):
            mine = (firsts[i] == 1) & (places[i] == k)
            owner_k = jnp.where(mine, owners[i], owner_k)
            partner_k = jnp.where(mine, partners[i], partner_k)
        owner_ref[k] = owner_k
        partner_ref[k] = partner_k
    return want_before, want_after


def kernel(
    n_tm,
    n_space,
    x_hbm,
    place_ref,
    rows_ref,
    counts_ref,
    out_ref,
    x_ref,
    pool_ref,
    turned_ref,
    part_ref,
    done_ref,
    sums_ref,
    first_ref,
    half_ref,
    second_ref,
    mean_ref,
    near_mean_ref,
    ask_ref,
    asked_ref,
    halo_out_ref,
    halo_in_ref,
    send_ref,
    recv_ref,
    slot_ref,
    owner_ref,
    partner_ref,
    load_sems,
    mean_sems,
    near_sems,
    ask_sems,
    halo_sems,
    ring_sems,
):
    z = lax.axis_index("tm")
    s = lax.axis_index("space")
    frames = x_ref.shape[2]
    slots = part_ref.shape[0]
    per_device = turned_ref.shape[0]
    rows = SPAN // n_tm
    steps = n_tm // 2
    groups = slots // GROUP
    quads = n_tm // 4
    before = (lax.rem(s + n_space - 1, n_space))
    after = lax.rem(s + 1, n_space)
    up = lax.rem(z + 1, n_tm)
    down = lax.rem(z + n_tm - 1, n_tm)
    near_z = [(z // 4) * 4 + lax.rem(z + r, 4) for r in range(1, 4)]
    far_z = [lax.rem(z + 4 * r, n_tm) for r in range(1, quads)]
    partners = [(z, before), (z, after), (up, s), (down, s)]
    partners += [(other, s) for other in near_z + far_z]

    def load(p):
        return pltpu.make_async_copy(x_hbm.at[:, :, p * BLK : (p + 1) * BLK], x_ref.at[p], load_sems.at[p])

    for p in range(per_device):
        load(p).start()

    barrier = pltpu.get_barrier_semaphore()
    for who in partners:
        pl.semaphore_signal(barrier, inc=1, device_id=who, device_id_type=MESH)

    want_before, want_after = plan(
        s, per_device, n_space, place_ref, rows_ref, counts_ref, slot_ref, owner_ref, partner_ref
    )
    ask_ref[0] = jnp.full(ask_ref.shape[1:], want_before, jnp.int32)
    ask_ref[1] = jnp.full(ask_ref.shape[1:], want_after, jnp.int32)
    pl.semaphore_wait(barrier, len(partners))

    def ask(side):
        return pltpu.make_async_remote_copy(
            src_ref=ask_ref.at[side],
            dst_ref=asked_ref.at[1 - side],
            send_sem=ask_sems.at[0, side],
            recv_sem=ask_sems.at[1, 1 - side],
            device_id=(z, (before, after)[side]),
            device_id_type=MESH,
        )

    for side in range(2):
        ask(side).start()

    sums_ref[...] = jnp.zeros_like(sums_ref)
    for p in range(per_device):
        load(p).wait()
        for c in range(COMPS):
            total = jnp.sum(x_ref[p, c].astype(jnp.float32), axis=0, keepdims=True)
            sums_ref[c * per_device + p : c * per_device + p + 1, :] = total

    def exchange(level, src, dst, slot, who, r):
        return pltpu.make_async_remote_copy(
            src_ref=src,
            dst_ref=dst.at[slot],
            send_sem=mean_sems.at[level, 0, r],
            recv_sem=mean_sems.at[level, 1, r],
            device_id=(who, s),
            device_id_type=MESH,
        )

    z_low, z_high = lax.rem(z, 4), z // 4
    for r, who in enumerate(near_z):
        exchange(0, sums_ref, first_ref, z_low, who, r).start()

    def halo(side, c):
        return pltpu.make_async_remote_copy(
            src_ref=halo_out_ref.at[side, c],
            dst_ref=halo_in_ref.at[1 - side, c],
            send_sem=halo_sems.at[0, side, c],
            recv_sem=halo_sems.at[1, 1 - side, c],
            device_id=(z, (before, after)[side]),
            device_id_type=MESH,
        )

    for side in range(2):
        ask(1 - side).wait_recv()
        wanted = jnp.clip(jnp.max(asked_ref[side]), 0, per_device - 1)
        for c in range(COMPS):
            halo_out_ref[side, c] = x_ref[wanted, c]
            halo(side, c).start()

    for r, who in enumerate(near_z):
        exchange(0, sums_ref, first_ref, z_low, who, r).wait_recv()
    first_ref[z_low] = sums_ref[...]
    half_ref[...] = (first_ref[0] + first_ref[1]) + (first_ref[2] + first_ref[3])
    for r, who in enumerate(far_z):
        exchange(1, half_ref, second_ref, z_high, who, r).start()
    for r, who in enumerate(far_z):
        exchange(1, half_ref, second_ref, z_high, who, r).wait_recv()
    second_ref[z_high] = half_ref[...]
    mean_sum = second_ref[0]
    for g in range(1, quads):
        mean_sum = mean_sum + second_ref[g]
    mean_ref[...] = mean_sum * (1.0 / (frames * n_tm))

    def near(side):
        return pltpu.make_async_remote_copy(
            src_ref=mean_ref,
            dst_ref=near_mean_ref.at[1 - side],
            send_sem=near_sems.at[0, side],
            recv_sem=near_sems.at[1, 1 - side],
            device_id=(z, (before, after)[side]),
            device_id_type=MESH,
        )

    for side in range(2):
        near(side).start()

    def centre_own(p, _):
        for c in range(COMPS):
            mean = mean_ref[pl.ds(c * per_device + p, 1), :]
            centred = (x_ref[p, c].astype(jnp.float32) - mean).astype(jnp.bfloat16)
            pool_ref[p, :, c * BLK : (c + 1) * BLK] = centred
            turned_ref[p, c] = centred.T
        return 0

    lax.fori_loop(0, per_device, centre_own, 0)

    def product(k, _):
        owner, partner = owner_ref[k], partner_ref[k]
        for c in range(COMPS):
            part_ref[k, c * BLK : (c + 1) * BLK, :] = jnp.dot(
                turned_ref[owner, c], pool_ref[partner], preferred_element_type=jnp.float32
            )
        return 0

    def length(way, g):
        return steps - (g + way) % 2

    def hop(way, k, g):
        return pltpu.make_async_remote_copy(
            src_ref=send_ref.at[way, k, g],
            dst_ref=recv_ref.at[way, k, g],
            send_sem=ring_sems.at[0, way, k, g],
            recv_sem=ring_sems.at[1, way, k, g],
            device_id=((up, down)[way], s),
            device_id_type=MESH,
        )

    def local(d, g):
        block = part_ref[g * GROUP : (g + 1) * GROUP, pl.ds(pl.multiple_of(d * rows, rows), rows), :]
        return block.reshape(GROUP * rows, SPAN)

    def forward(k, g, fresh):
        for way in range(2):
            ahead = length(way, g) - k
            target = lax.rem(z + n_tm + (ahead if way == 0 else -ahead), n_tm)
            value = local(target, g)
            if not fresh:
                hop(way, k - 1, g).wait_recv()
                value = value + recv_ref[way, k - 1, g].astype(jnp.float32)
            send_ref[way, k, g] = value.astype(jnp.bfloat16)
            hop(way, k, g).start()

    early = EARLY // GROUP
    for g in range(early):
        lax.fori_loop(g * GROUP, (g + 1) * GROUP, product, 0)
        forward(0, g, True)
    for g in range(early):
        forward(1, g, False)

    for side in range(2):
        near(side).wait_recv()
    for side in range(2):
        wanted = (want_before, want_after)[side]
        for c in range(COMPS):
            halo(1 - side, c).wait_recv()
            mean = near_mean_ref[side, c * per_device + wanted][None, :]
            centred = (halo_in_ref[side, c].astype(jnp.float32) - mean).astype(jnp.bfloat16)
            pool_ref[per_device + side, :, c * BLK : (c + 1) * BLK] = centred

    for g in range(early, groups):
        lax.fori_loop(g * GROUP, (g + 1) * GROUP, product, 0)
        forward(0, g, True)
    for g in range(early, groups):
        forward(1, g, False)

    def middle(k, _):
        for g in range(groups):
            forward(k, g, False)
        return 0

    lax.fori_loop(2, steps - 1, middle, 0)

    for g in range(groups):
        way = g % 2
        last = steps - 1
        target = up if way == 0 else down
        hop(way, last - 1, g).wait_recv()
        value = local(target, g) + recv_ref[way, last - 1, g].astype(jnp.float32)
        send_ref[way, last, g] = value.astype(jnp.bfloat16)
        hop(way, last, g).start()
    for g in range(groups):
        value = local(z, g)
        for way in (1 - g % 2, g % 2):
            last = length(way, g) - 1
            hop(way, last, g).wait_recv()
            value = value + recv_ref[way, last, g].astype(jnp.float32)
        done_ref[g * GROUP : (g + 1) * GROUP] = value.reshape(GROUP, rows, SPAN)

    scale = 1.0 / (frames * n_tm)
    for i in range(slots):
        weight = jnp.where(i < counts_ref[0], jnp.float32(scale), jnp.float32(0.0))
        out_ref[i] = done_ref[slot_ref[i]] * weight

    for side in range(2):
        ask(side).wait_send()
        near(side).wait_send()
        for c in range(COMPS):
            halo(side, c).wait_send()
    for r, who in enumerate(near_z):
        exchange(0, sums_ref, first_ref, z_low, who, r).wait_send()
    for r, who in enumerate(far_z):
        exchange(1, half_ref, second_ref, z_high, who, r).wait_send()

    def drain(k, _):
        for g in range(groups):
            for way in range(2):
                hop(way, k, g).wait_send()
        return 0

    lax.fori_loop(0, steps - 1, drain, 0)
    for g in range(groups):
        hop(g % 2, steps - 1, g).wait_send()


def body(n_tm, n_space, displacements, block_place, pair_list, counts):
    frames, atoms = displacements.shape[1:]
    per_device = atoms // BLK
    slots = pair_list.shape[0]
    rows = SPAN // n_tm
    steps, groups = n_tm // 2, slots // GROUP
    bf16, f32, i32 = jnp.bfloat16, jnp.float32, jnp.int32
    smem = pl.BlockSpec(memory_space=pltpu.SMEM)
    result = pl.pallas_call(
        functools.partial(kernel, n_tm, n_space),
        out_shape=jax.ShapeDtypeStruct((slots, rows, SPAN), f32),
        in_specs=[pl.BlockSpec(memory_space=pl.ANY), smem, smem, smem],
        out_specs=pl.BlockSpec(memory_space=pltpu.VMEM),
        scratch_shapes=[
            pltpu.VMEM((per_device, COMPS, frames, BLK), bf16),
            pltpu.VMEM((per_device + 2, frames, SPAN), bf16),
            pltpu.VMEM((per_device, COMPS, BLK, frames), bf16),
            pltpu.VMEM((slots, SPAN, SPAN), f32),
            pltpu.VMEM((slots, rows, SPAN), f32),
            pltpu.VMEM((16, BLK), f32),
            pltpu.VMEM((4, 16, BLK), f32),
            pltpu.VMEM((16, BLK), f32),
            pltpu.VMEM((n_tm // 4, 16, BLK), f32),
            pltpu.VMEM((16, BLK), f32),
            pltpu.VMEM((2, 16, BLK), f32),
            pltpu.VMEM((2, 8, BLK), i32),
            pltpu.VMEM((2, 8, BLK), i32),
            pltpu.VMEM((2, COMPS, frames, BLK), bf16),
            pltpu.VMEM((2, COMPS, frames, BLK), bf16),
            pltpu.VMEM((2, steps, groups, GROUP * rows, SPAN), bf16),
            pltpu.VMEM((2, steps, groups, GROUP * rows, SPAN), bf16),
            pltpu.SMEM((slots,), i32),
            pltpu.SMEM((slots,), i32),
            pltpu.SMEM((slots,), i32),
            pltpu.SemaphoreType.DMA((per_device,)),
            pltpu.SemaphoreType.DMA((2, 2, 3)),
            pltpu.SemaphoreType.DMA((2, 2)),
            pltpu.SemaphoreType.DMA((2, 2)),
            pltpu.SemaphoreType.DMA((2, 2, COMPS)),
            pltpu.SemaphoreType.DMA((2, 2, steps, groups)),
        ],
        compiler_params=pltpu.CompilerParams(
            collective_id=0, has_side_effects=True, vmem_limit_bytes=56 * 1024 * 1024
        ),
    )(displacements, block_place, pair_list, counts)
    return jnp.transpose(result, (1, 0, 2))


def solution(mesh):
    in_specs = (P(None, "tm", "space"), P(), P("space", None), P("space"))
    return jax.shard_map(
        functools.partial(body, mesh.shape["tm"], mesh.shape["space"]),
        mesh=mesh,
        in_specs=in_specs,
        out_specs=P("tm", "space", None),
        check_vma=False,
    )
```

time: 405 us -> 78 us (0.19)
  waiting for transfers between devices: 196 us -> 0 us
  Pallas kernels: 0 us -> 74 us
  loops' own time: 46.1 us -> 0 us
  matrix products: 41.2 us -> 0 us
  blocking collectives: 36.3 us -> 0 us
  local copies, waits for them, and re-layouts: 36.2 us -> 3.16 us
  starting transfers between devices: 18.8 us -> 0 us
  between operations: 18.3 us -> 0.66 us
  other arithmetic: 8.67 us -> 0 us
    psum x1 -> x0, waiting for transfers between devices: 188 us -> none  [body(): lax.psum(lax.fori_loop(0, slot_total, accumulate, start_value), 'tm')]
    pallas_call x0 -> x1, Pallas kernels: none -> 74 us  [body(): pl.pallas_call(functools.partial(kernel, n_tm, n_space), out_shape=jax.Sh...]
    another operation x1 -> x0, loops' own time: 46.1 us -> none  [body(): lax.fori_loop(0, slot_total, accumulate, start_value)]
    dot_general x12 -> x0, matrix products: 41.2 us -> none  [pair_product(): lax.dot_general(owner_rows, block_pool[partner_pos[slot_index]], (((0,),...]
    psum x1 -> x0, blocking collectives: 36.3 us -> none  [body(): frame_mean = lax.psum(frame_sums, 'tm') * inverse_frames]
    dynamic_slice x38 -> x0, local copies, waits for them, and re-layouts: 24.6 us -> none  [the longest x12 7.41 us: pair_product(): partner_pos[slot_index]]
    ppermute x6 -> x0, starting transfers between devices: 18.8 us -> none  [from_behind(): return lax.ppermute(value, axis, pairs)]
    ppermute x6 -> x0, waiting for transfers between devices: 8.4 us -> none  [from_behind(): return lax.ppermute(value, axis, pairs)]
  transfers between devices with their start and end apart: 7 -> 0, of which waited for: 3 -> 0; matrix products, arithmetic and copies ran while one was open for 2% -> 0% of each run, Pallas kernels for 0% -> 0%
where the time goes in v1:
time: 78 us; the launch traced here: 77.8 us
  Pallas kernels  74 us (95%)
  local copies, waits for them, and re-layouts  3.16 us (4%)
    pallas_call x1, Pallas kernels, body(): pl.pallas_call(functools.partial(kernel, n_tm, n_space), out_shape=jax.Sh...  74 us
    unnamed x2, local copies, waits for them, and re-layouts  3.16 us

profile of v1, /device:TPU:30, one launch (start us, length us, event | category | flops | bytes accessed | tf_op | source)
XLA Modules:
  0.0 77.8 jit_solution(4188322170070619893)
XLA Ops:
  0.7 1.4 %copy.5.rows_ref = s32[12,2]{1,0:T(8,128)} copy(s32[12,2]{0,1:T(2,128)} %param.6) | data formatting | bytes 192 | tf_op args[2]
  2.0 74.0 %shard_map.46 = f32[12,24,384]{2,1,0:T(8,128)} custom-call(bf16[3,1024,512]{2,1,0:T(8,128)(2,1)} %x_hbm.1, s32[128]{0:T(128)} %place_ref.1, s32[12,2]{1,0:T(8,128)} %copy.5.rows_ref, s32[1]{0:T(128)S(6)} %copy.7.counts_ref), custom_call_target="tpu_custom_call" | custom-call | tf_op jit(solution)/shard_map/pallas_call | solution.py:339
  76.0 1.8 %copy.8 = f32[24,12,384]{2,0,1:T(8,128)} copy(f32[24,12,384]{2,0,1:T(8,128)} %bitcast.1) | data formatting | bytes 884736
